TPU v7x, 128 devices: a whole 4x4x4 slice. The times are simulated.
128 devices in a mesh: grp: 4 (over x), gx: 4 (over z_lo, core), gy: 8 (over z_hi, y).
Axes of the slice: x: 4, y: 4, z: 4 (z_hi: 2, z_lo: 2; z = z_hi * 2 + z_lo), core: 2. Of those that a mesh axis runs over, the one named last changes fastest.
Arguments:
- flow_state: float32 [8, 768, 128, 128], P(None, ('grp', 'gx'), 'gy'), may hold values from -90 to 90
- speeds: float32 [3, 8], replicated, may hold values from 0.3 to 1.2
- viscosity: float32 [8], replicated, may hold values from 0.02 to 0.2
- reaction: float32 [8, 8], replicated, may hold values from -2 to 2
- start_basis: float32 [768, 96], replicated, may hold values from -6 to 6
- slab_table: int32 [8, 8, 1], replicated, may hold values from 0 to 15; in each aligned block of 8 rows (0 to 7, 8 to 15, ..., all dimensions but the last counted through in order) at most 2 rows name the same one
Outputs:
- final_state: float32 [8, 768, 128, 128], P(None, ('grp', 'gx'), 'gy')
- core_slots: float32 [256, 96, 8, 2, 128], P(('grp', 'gx', 'gy'))
Inputs may be any that keep to these rules, and one draw needn't show every extreme that they name: slab_table[t, u, 0] names the slab that stores unit u of row t; within each row t no slab is named by more than 2 units, a bound that some block reaches.
All inputs are finite; a program needn't handle non-finite values.
Results may differ from a plain program's by a relative error of at most 0.0034.
Values may be sent and summed in bfloat16 or wider, within the bound.
A program may use at most 256 MiB of HBM per device.

v0:
```python
import jax
import jax.numpy as jnp
from jax import lax
from jax.sharding import PartitionSpec as P

V = 8
NX = 768
R = 96
NZ = 128
YB = 2
NEWTON = 5
slope_weights = (0.8, -0.2, 4.0 / 105.0, -1.0 / 280.0)
curve_weights = (1.6, -0.2, 8.0 / 315.0, -1.0 / 560.0)
curve_center = -205.0 / 72.0
time_step = 0.2


def extended(shard, sides, width):
    for axis, dim in sides:
        peers, length = (lax.axis_size(axis), shard.shape[dim])
        up = [(i, (i + 1) % peers) for i in range(peers)]
        down = [(j, i) for i, j in up]
        last = lax.slice_in_dim(shard, length - width, length, axis=dim)
        initial = lax.slice_in_dim(shard, 0, width, axis=dim)
        before = lax.ppermute(last, axis, up)
        after = lax.ppermute(initial, axis, down)
        shard = jnp.concatenate([before, shard, after], axis=dim)
    return shard


def tendency(padded, speeds, viscosity, reaction):
    center = padded[:, 4:-4, 4:-4, :]
    width_first = center.shape[1]
    width_second = center.shape[2]
    diffusion = viscosity[:, None, None, None]
    speed_one = speeds[0][:, None, None, None]
    speed_two = speeds[1][:, None, None, None]
    speed_three = speeds[2][:, None, None, None]
    summed = 3.0 * curve_center * diffusion * center
    summed = summed + jnp.einsum("kj,jxyz->kxyz", reaction, center, precision=lax.Precision.HIGHEST)
    for offset in range(1, 5):
        slope_weight = slope_weights[offset - 1]
        curve_weight = curve_weights[offset - 1]
        spread = curve_weight * diffusion
        summed = summed + (
            (spread - slope_weight * speed_one)
            * padded[:, 4 + offset : 4 + offset + width_first, 4 : 4 + width_second, :]
            + (spread + slope_weight * speed_one)
            * padded[:, 4 - offset : 4 - offset + width_first, 4 : 4 + width_second, :]
            + (spread - slope_weight * speed_two)
            * padded[:, 4 : 4 + width_first, 4 + offset : 4 + offset + width_second, :]
            + (spread + slope_weight * speed_two)
            * padded[:, 4 : 4 + width_first, 4 - offset : 4 - offset + width_second, :]
            + (spread - slope_weight * speed_three) * jnp.roll(center, -offset, 3)
            + (spread + slope_weight * speed_three) * jnp.roll(center, offset, 3)
        )
    return summed


def extend(field):
    return extended(field, ((("grp", "gx"), 1), ("gy", 2)), 4)


def on_device(flow_state, speeds, viscosity, reaction, start_basis, slab_table):
    first = flow_state + time_step * tendency(extend(flow_state), speeds, viscosity, reaction)
    final_state = 0.5 * flow_state + 0.5 * (
        first + time_step * tendency(extend(first), speeds, viscosity, reaction)
    )
    snapshot = final_state.astype(jnp.bfloat16)
    tile_rows = flow_state.shape[1]
    unit_count = flow_state.shape[2] // YB
    slab_count = lax.axis_size(("grp", "gx"))
    capacity = max(2, 3 * unit_count // slab_count)
    columns = V * YB * NZ
    table_row = lax.dynamic_index_in_dim(
        slab_table[:, :, 0], lax.axis_index("gy"), 0, keepdims=False
    )
    order = jnp.arange(unit_count, dtype=jnp.int32)
    earlier = order[None, :] < order[:, None]
    same_slab = table_row[:, None] == table_row[None, :]
    slot_index = jnp.sum((same_slab & earlier).astype(jnp.int32), axis=1)
    target = table_row * capacity + slot_index
    placing = (
        jnp.arange(slab_count * capacity, dtype=jnp.int32)[:, None] == target[None, :]
    ).astype(jnp.bfloat16)
    blocks = snapshot.reshape(V, tile_rows, unit_count, YB, NZ)
    outgoing = jnp.einsum(
        "pu,vxuyz->pxvyz", placing, blocks, preferred_element_type=jnp.float32
    ).astype(jnp.bfloat16)
    received = lax.all_to_all(
        outgoing.reshape(slab_count, capacity, tile_rows, columns),
        ("grp", "gx"),
        split_axis=0,
        concat_axis=2,
        tiled=True,
    )
    received = received.reshape(capacity, NX, columns)
    partial_value = lax.dot_general(
        received, received, (((0, 2), (0, 2)), ((), ())), preferred_element_type=jnp.float32
    )
    gram = lax.psum(partial_value, ("grp", "gx", "gy"))
    product = jnp.dot(gram, start_basis, precision=lax.Precision.HIGHEST)
    basis = product / jnp.sqrt(jnp.sum(product * product))
    for repeat in range(NEWTON):
        inner_gram = jnp.dot(basis.T, basis, precision=lax.Precision.HIGHEST)
        basis = 1.5 * basis - 0.5 * jnp.dot(basis, inner_gram, precision=lax.Precision.HIGHEST)
    basis_half = basis.astype(jnp.bfloat16)
    cores = jnp.einsum("xr,mxc->mrc", basis_half, received, preferred_element_type=jnp.float32)
    return (final_state, cores.reshape(capacity, R, V, YB, NZ))


def solution(mesh):
    placed = (P(None, ("grp", "gx"), "gy", None), P(), P(), P(), P(), P())
    return jax.shard_map(
        on_device,
        mesh=mesh,
        in_specs=placed,
        out_specs=(
            P(None, ("grp", "gx"), "gy", None),
            P(("grp", "gx", "gy"), None, None, None, None),
        ),
        check_vma=False,
    )
```

profile of v0, /device:TPU:1, one launch (start us, length us, event | category | flops | bytes accessed | tf_op | source)
XLA Modules:
  0.0 518.8 jit_solution(14506563445527793642)
XLA Ops:
  13.1 5.8 %fusion.114 = (f32[8,48,16,1]{3,2,1,0:T(8,128)S(1)}, f32[8,48,16,1]{3,2,1,0:T(8,128)}) fusion(f32[8,48,16,128]{3,2,1,0:T(8,128)} %param.6), kind=kLoop, calls=%fused_computation.230 | loop fusion | bytes 98304 | tf_op jit(solution)/shard_map/jit(_roll_static)/slice | solution.py:55
  18.9 3.9 fusion.115
  32.6 5.7 %constant_dynamic-update-slice_fusion.1 = (f32[8,52,16,128]{3,0,2,1:T(8,128)}, f32[8,52,16,128]{3,0,2,1:T(8,128)}, f32[8,56,16,128]{3,0,2,1:T(8,128)}) fusion(f32[8,48,16,128]{3,2,1,0:T(8,128)S(1)} %copy-done.1, f32[8,52,16,128]{3,0,2,1:T(8,128)} %get-tuple-element.55, f32[8,56,16,128]{3,0,2,1:T(8,128)} %get-tuple-element.56), kind=kLoop, calls=%fused_computation.168 | loop fusion | bytes 12582912
  42.0 5.8 %collective-permute-start.2 = (f32[8,56,4,128]{3,0,2,1:T(8,128)}, f32[8,56,4,128]{3,0,2,1:T(8,128)}, u32[]{:S(2)}, u32[]{:S(2)}) collective-permute-start(f32[8,56,4,128]{3,0,2,1:T(8,128)} %get-tuple-element.12), channel_id=1, source_target_pairs={{1,0},{2,1},{3,2},{4,3},{5,4},{6,5},{7,6},{0,7},{9,8},{10,9},{11,1... | collective-permute-start | bytes 2752520 | tf_op jit(solution)/shard_map/ppermute | solution.py:26
  51.7 5.6 %copy.105 = f32[8,48,16,1]{3,0,2,1:T(8,128)} copy(f32[8,48,16,1]{3,2,1,0:T(8,128)} %get-tuple-element.45) | data formatting | bytes 49152
  92.4 3.8 copy.116
  111.7 37.7 %fusion.43 = f32[8,48,16,128]{3,0,2,1:T(8,128)S(1)} fusion(f32[8,56,16,128]{3,0,2,1:T(8,128)} %get-tuple-element.54, f32[8,56,4,128]{3,0,2,1:T(8,128)} %collective-permute-done.3, f32[8,56,4,128]{3,0,2,1:T(8,128)} %collective-permute-done.2, f32[8,52,16,128]{3,0,2,1:T(8,128)} %get-tuple-element.49, f32[8,52,16,128]{3,0,2,1:T(8,128)} %get-tuple-element.53, ...), kind=kOutput, calls=%fused_computation.70 | convolution fusion | flops 128974848 | bytes 90440736 | tf_op jit(solution)/shard_map/kj,jxyz->kxyz/dot_general | solution.py:40
  153.3 3.8 fusion.100
  157.1 3.8 fusion.101
  161.0 3.9 fusion.102
  171.4 3.9 fusion.104
  177.6 5.4 %collective-permute-start.6 = (f32[8,56,4,128]{3,0,2,1:T(8,128)S(1)}, f32[8,56,4,128]{3,0,2,1:T(8,128)S(1)}, u32[]{:S(2)}, u32[]{:S(2)}) collective-permute-start(f32[8,56,4,128]{3,0,2,1:T(8,128)S(1)} %get-tuple-element.10), channel_id=1, source_target_pairs={{1,0},{2,1},{3,2},{4,3},{5,4},{6,5},{7,6},{0,7},{9,8},{10,9},{11,1... | collective-permute-start | bytes 2752520 | tf_op jit(solution)/shard_map/ppermute | solution.py:26
  187.0 3.9 fusion.106
  190.8 9.9 %collective-permute-done.6 = f32[8,56,4,128]{3,0,2,1:T(8,128)S(1)} collective-permute-done((f32[8,56,4,128]{3,0,2,1:T(8,128)S(1)}, f32[8,56,4,128]{3,0,2,1:T(8,128)S(1)}, u32[]{:S(2)}, u32[]{:S(2)}) %collective-permute-start.6) | collective-permute-done | bytes 917536 | tf_op jit(solution)/shard_map/ppermute | solution.py:26
  200.8 5.7 %collective-permute-done.7 = f32[8,56,4,128]{3,0,2,1:T(8,128)S(1)} collective-permute-done((f32[8,56,4,128]{3,0,2,1:T(8,128)S(1)}, f32[8,56,4,128]{3,0,2,1:T(8,128)S(1)}, u32[]{:S(2)}, u32[]{:S(2)}) %collective-permute-start.7) | collective-permute-done | bytes 917536 | tf_op jit(solution)/shard_map/ppermute | solution.py:25
  206.5 3.9 pad_maximum_fusion
  210.4 25.6 %fusion.117 = (bf16[8,48,16,128]{3,0,2,1:T(8,128)(2,1)S(1)}, f32[8,48,16,128]{3,0,2,1:T(8,128)}) fusion(f32[8,48,16,128]{3,0,2,1:T(8,128)S(1)} %fusion.43, f32[8,48,16,124]{3,0,2,1:T(8,128)} %get-tuple-element.16, f32[8,48,16,4]{3,0,2,1:T(8,128)} %get-tuple-element.14, f32[8]{0:T(128)S(1)} %get-tuple-element.62, f32[8,48,16,4]{3,0,2,1:T(8,128)} %get-tuple-element.15, ...), kind=kOutput, calls=%fused_computation.233 | convolution fusion | flops 131334144 | bytes 65028608 | tf_op jit(solution)/shard_map/kj,jxyz->kxyz/dot_general | solution.py:40
  237.9 10.6 %copy.90 = bf16[32,48,8,2,128]{4,3,2,1,0:T(2,128)(2,1)} copy(bf16[32,48,8,2,128]{4,0,3,1,2:T(8,128)(2,1)S(1)} %convert_bitcast_fusion) | data formatting | bytes 12582912 | tf_op jit(solution)/shard_map/convert_element_type | solution.py:89
  248.6 11.1 %reshape.133 = bf16[16,2,48,2048]{3,2,1,0:T(8,128)(2,1)} reshape(bf16[32,48,8,2,128]{4,3,2,1,0:T(2,128)(2,1)} %copy.90) | data formatting | bytes 12582912 | tf_op jit(solution)/shard_map/reshape | solution.py:91
  259.7 78.8 %all_to_all.15 = bf16[16,2,48,2048]{3,2,1,0:T(8,128)(2,1)S(1)} all-to-all(bf16[16,2,48,2048]{3,2,1,0:T(8,128)(2,1)} %reshape.133), channel_id=1, replica_groups=mesh['grp'=4,'gx'=4,'gy'=8] {'grp','gx'}, dimensions={0} | all-to-all | bytes 12582912 | tf_op jit(solution)/shard_map/all_to_all | solution.py:90
  342.3 6.5 %convolution_bitcast_fusion.1 = f32[768,768]{1,0:T(8,128)} fusion(bf16[2,768,2048]{2,1,0:T(8,128)(2,1)S(1)} %bitcast.95), kind=kOutput, calls=%fused_computation.147 | convolution fusion | flops 4831838208 | bytes 8650752 | tf_op jit(solution)/shard_map/dot_general | solution.py:98
  351.0 144.7 %all-reduce.2.cloned.1.call-done = f32[768,768]{1,0:T(8,128)} async-done(((f32[768,768]{1,0:T(8,128)}), f32[768,768]{1,0:T(8,128)}) %all-reduce.2.cloned.1.call-update) | async-done | bytes 2359312 | tf_op jit(solution)/shard_map/psum | solution.py:101
  495.8 4.6 multiply_reduce_fusion
  505.4 4.0 convolution_bitcast_fusion
  (96 shorter events, 105.2 us)
Async XLA Ops:
  7.2 488.6 %copy-start = (f32[768,96]{0,1:T(8,128)S(1)}, f32[768,96]{0,1:T(8,128)}, u32[]{:S(2)}) copy-start(f32[768,96]{0,1:T(8,128)} %param.10) | copy-start | bytes 884740
  7.2 488.6 %all-reduce.2.cloned.1.call-start = ((), (), s32[]{:S(2)}) async-start(), calls=%async_computation.1 | async-start | bytes 4718592 | tf_op jit(solution)/shard_map/psum | solution.py:101
  9.2 21.6 %collective-permute-start.1 = (f32[8,4,16,128]{3,0,2,1:T(8,128)}, f32[8,4,16,128]{3,0,2,1:T(8,128)}, u32[]{:S(2)}, u32[]{:S(2)}) collective-permute-start(f32[8,4,16,128]{3,0,2,1:T(8,128)} %copy.103), channel_id=1, source_target_pairs={{0,8},{8,16},{16,24},{24,32},{32,40},{40,48},{48,56},{56,64},{64,7... | collective-permute-start | bytes 786440 | tf_op jit(solution)/shard_map/ppermute | solution.py:25
  13.1 5.8 %copy-start.1 = (f32[8,48,16,128]{3,2,1,0:T(8,128)S(1)}, f32[8,48,16,128]{3,2,1,0:T(8,128)}, u32[]{:S(2)}) copy-start(f32[8,48,16,128]{3,2,1,0:T(8,128)} %param.6) | copy-start | bytes 9437188
  13.1 25.2 %collective-permute-start = (f32[8,4,16,128]{3,0,2,1:T(8,128)}, f32[8,4,16,128]{3,0,2,1:T(8,128)S(1)}, u32[]{:S(2)}, u32[]{:S(2)}) collective-permute-start(f32[8,4,16,128]{3,0,2,1:T(8,128)} %copy.104), channel_id=1, source_target_pairs={{8,0},{16,8},{24,16},{32,24},{40,32},{48,40},{56,48},{64,56},{72,6... | collective-permute-start | bytes 786440 | tf_op jit(solution)/shard_map/ppermute | solution.py:26
  42.0 69.7 %collective-permute-start.2 = (f32[8,56,4,128]{3,0,2,1:T(8,128)}, f32[8,56,4,128]{3,0,2,1:T(8,128)}, u32[]{:S(2)}, u32[]{:S(2)}) collective-permute-start(f32[8,56,4,128]{3,0,2,1:T(8,128)} %get-tuple-element.12), channel_id=1, source_target_pairs={{1,0},{2,1},{3,2},{4,3},{5,4},{6,5},{7,6},{0,7},{9,8},{10,9},{11,1... | collective-permute-start | bytes 2752520 | tf_op jit(solution)/shard_map/ppermute | solution.py:26
  47.8 63.9 %collective-permute-start.3 = (f32[8,56,4,128]{3,0,2,1:T(8,128)}, f32[8,56,4,128]{3,0,2,1:T(8,128)}, u32[]{:S(2)}, u32[]{:S(2)}) collective-permute-start(f32[8,56,4,128]{3,0,2,1:T(8,128)} %get-tuple-element.13), channel_id=1, source_target_pairs={{0,1},{1,2},{2,3},{3,4},{4,5},{5,6},{6,7},{7,0},{8,9},{9,10},{10,1... | collective-permute-start | bytes 2752520 | tf_op jit(solution)/shard_map/ppermute | solution.py:25
  51.7 5.6 %copy-start.7 = (f32[8,48,16,127]{3,2,1,0:T(8,128)S(1)}, f32[8,48,16,127]{3,2,1,0:T(8,128)}, u32[]{:S(2)}) copy-start(f32[8,48,16,127]{3,2,1,0:T(8,128)} %get-tuple-element.47) | copy-start | bytes 9363460
  57.3 3.5 copy-start.6
  67.8 3.6 copy-start.5
  71.4 3.7 copy-start.4
  96.2 3.5 copy-start.9
  99.7 3.4 copy-start.8
  106.7 4.9 copy-start.13
  106.7 4.9 copy-start.14
  106.7 5.0 copy-start.15
  168.6 6.6 %collective-permute-start.4 = (f32[8,4,16,128]{3,0,2,1:T(8,128)S(1)}, f32[8,4,16,128]{3,0,2,1:T(8,128)S(1)}, u32[]{:S(2)}, u32[]{:S(2)}) collective-permute-start(f32[8,4,16,128]{3,0,2,1:T(8,128)S(1)} %get-tuple-element.30), channel_id=1, source_target_pairs={{8,0},{16,8},{24,16},{32,24},{40,32},{48,40},{56,48},{64,56},{72,6... | collective-permute-start | bytes 786440 | tf_op jit(solution)/shard_map/ppermute | solution.py:26
  171.4 6.0 %collective-permute-start.5 = (f32[8,4,16,128]{3,0,2,1:T(8,128)S(1)}, f32[8,4,16,128]{3,0,2,1:T(8,128)S(1)}, u32[]{:S(2)}, u32[]{:S(2)}) collective-permute-start(f32[8,4,16,128]{3,0,2,1:T(8,128)S(1)} %get-tuple-element.31), channel_id=1, source_target_pairs={{0,8},{8,16},{16,24},{24,32},{32,40},{40,48},{48,56},{56,64},{64,7... | collective-permute-start | bytes 786440 | tf_op jit(solution)/shard_map/ppermute | solution.py:25
  175.3 31.2 %copy-start.11 = (f32[8,4,16,128]{3,0,2,1:T(8,128)}, f32[8,4,16,128]{3,0,2,1:T(8,128)S(1)}, u32[]{:S(2)}) copy-start(f32[8,4,16,128]{3,0,2,1:T(8,128)S(1)} %collective-permute-done.4) | copy-start | bytes 786436
  177.4 29.1 %copy-start.12 = (f32[8,4,16,128]{3,0,2,1:T(8,128)}, f32[8,4,16,128]{3,0,2,1:T(8,128)S(1)}, u32[]{:S(2)}) copy-start(f32[8,4,16,128]{3,0,2,1:T(8,128)S(1)} %collective-permute-done.5) | copy-start | bytes 786436
  177.6 23.2 %collective-permute-start.6 = (f32[8,56,4,128]{3,0,2,1:T(8,128)S(1)}, f32[8,56,4,128]{3,0,2,1:T(8,128)S(1)}, u32[]{:S(2)}, u32[]{:S(2)}) collective-permute-start(f32[8,56,4,128]{3,0,2,1:T(8,128)S(1)} %get-tuple-element.10), channel_id=1, source_target_pairs={{1,0},{2,1},{3,2},{4,3},{5,4},{6,5},{7,6},{0,7},{9,8},{10,9},{11,1... | collective-permute-start | bytes 2752520 | tf_op jit(solution)/shard_map/ppermute | solution.py:26
  183.0 23.5 %collective-permute-start.7 = (f32[8,56,4,128]{3,0,2,1:T(8,128)S(1)}, f32[8,56,4,128]{3,0,2,1:T(8,128)S(1)}, u32[]{:S(2)}, u32[]{:S(2)}) collective-permute-start(f32[8,56,4,128]{3,0,2,1:T(8,128)S(1)} %get-tuple-element.11), channel_id=1, source_target_pairs={{0,1},{1,2},{2,3},{3,4},{4,5},{5,6},{6,7},{7,0},{8,9},{9,10},{10,1... | collective-permute-start | bytes 2752520 | tf_op jit(solution)/shard_map/ppermute | solution.py:25
  190.8 19.6 %copy-start.2 = (f32[8,48,16,128]{3,2,1,0:T(8,128)S(1)}, f32[8,48,16,128]{3,2,1,0:T(8,128)}, u32[]{:S(2)}) copy-start(f32[8,48,16,128]{3,2,1,0:T(8,128)} %param.6) | copy-start | bytes 9437188
  342.3 6.5 %copy-start.10 = (f32[8,48,16,128]{3,0,2,1:T(8,128)S(1)}, f32[8,48,16,128]{3,0,2,1:T(8,128)}, u32[]{:S(2)}) copy-start(f32[8,48,16,128]{3,0,2,1:T(8,128)} %get-tuple-element.83) | copy-start | bytes 9437188
  (1 other events, 2.7 us)
Sparse Core Ops, SparseCore 0:
  348.9 146.8 all-reduce.1
where the time goes:
time: 528 us; the launch traced here: 519 us
  waiting for transfers between devices  163 us (31%)
  local copies, waits for them, and re-layouts  155 us (29%)
  matrix products  84.6 us (16%)
  blocking collectives  78.8 us (15%)
  starting transfers between devices  17.4 us (3%)
  between operations  15.1 us (3%)
    psum x1, waiting for transfers between devices, on_device(): gram = lax.psum(partial_value, ('grp', 'gx', 'gy'))  145 us
    all_to_all x1, blocking collectives, on_device(): lax.all_to_all(outgoing.reshape(slab_count, capacity, tile_rows, columns)...  78.8 us
    unnamed x53, local copies, waits for them, and re-layouts  72.6 us
    dot_general x2, matrix products, tendency(): jnp.einsum('kj,jxyz->kxyz', reaction, center, precision=lax.Precision.HIG...  63.4 us
    slice x16, local copies, waits for them, and re-layouts, tendency(): jnp.roll(center, offset, 3)  52 us
    ppermute x4, starting transfers between devices, extended(): after = lax.ppermute(initial, axis, down)  13.9 us
    reshape x1, local copies, waits for them, and re-layouts, on_device(): outgoing.reshape(slab_count, capacity, tile_rows, columns)  11.1 us
    convert_element_type x1, local copies, waits for them, and re-layouts, on_device(): outgoing = jnp.einsum('pu,vxuyz->pxvyz', placing, blocks, preferred_eleme...  10.6 us
  transfers between devices with their start and end apart: 9, of which 4 were waited for; matrix products, arithmetic and copies ran while one was open for 20% of the time, Pallas kernels for 0%

commit v1 on v0

--- a/solution.py
+++ b/solution.py
@@ -98,7 +98,7 @@
     partial_value = lax.dot_general(
         received, received, (((0, 2), (0, 2)), ((), ())), preferred_element_type=jnp.float32
     )
-    gram = lax.psum(partial_value, ("grp", "gx", "gy"))
+    gram = lax.psum(lax.psum(partial_value, "grp"), ("gx", "gy"))
     product = jnp.dot(gram, start_basis, precision=lax.Precision.HIGHEST)
     basis = product / jnp.sqrt(jnp.sum(product * product))
     for repeat in range(NEWTON):

time: 528 us -> 550 us (1.042)
  waiting for transfers between devices: 163 us -> 185 us
    psum x1 -> x2, waiting for transfers between devices: 145 us -> 167 us  [on_device(): gram = lax.psum(lax.psum(partial_value, 'grp'), ('gx', 'gy'))]
  transfers between devices with their start and end apart: 9 -> 10, of which waited for: 4 -> 5; matrix products, arithmetic and copies ran while one was open for 20% -> 19% of each run, Pallas kernels for 0% -> 0%
where the time goes in v1:
time: 550 us; the launch traced here: 542 us
  waiting for transfers between devices  185 us (34%)
  local copies, waits for them, and re-layouts  155 us (28%)
  matrix products  84.4 us (15%)
  blocking collectives  78.9 us (14%)
  starting transfers between devices  17.6 us (3%)
  between operations  15.2 us (3%)
    psum x2, waiting for transfers between devices, on_device(): gram = lax.psum(lax.psum(partial_value, 'grp'), ('gx', 'gy'))  167 us
    all_to_all x1, blocking collectives, on_device(): lax.all_to_all(outgoing.reshape(slab_count, capacity, tile_rows, columns)...  78.9 us
    unnamed x53, local copies, waits for them, and re-layouts  72.6 us
    dot_general x2, matrix products, tendency(): jnp.einsum('kj,jxyz->kxyz', reaction, center, precision=lax.Precision.HIG...  63.2 us
    slice x16, local copies, waits for them, and re-layouts, tendency(): jnp.roll(center, offset, 3)  52 us
    ppermute x4, starting transfers between devices, extended(): after = lax.ppermute(initial, axis, down)  13.9 us
    reshape x1, local copies, waits for them, and re-layouts, on_device(): outgoing.reshape(slab_count, capacity, tile_rows, columns)  11.1 us
  transfers between devices with their start and end apart: 10, of which 5 were waited for; matrix products, arithmetic and copies ran while one was open for 19% of the time, Pallas kernels for 0%

profile of v1, /device:TPU:1, one launch (start us, length us, event | category | flops | bytes accessed | tf_op | source)
XLA Modules:
  0.0 541.7 jit_solution(7834578523250096994)
XLA Ops:
  13.1 5.8 %fusion.114 = (f32[8,48,16,1]{3,2,1,0:T(8,128)S(1)}, f32[8,48,16,1]{3,2,1,0:T(8,128)}) fusion(f32[8,48,16,128]{3,2,1,0:T(8,128)} %param.6), kind=kLoop, calls=%fused_computation.230 | loop fusion | bytes 98304 | tf_op jit(solution)/shard_map/jit(_roll_static)/slice | solution.py:55
  18.9 3.9 fusion.115
  32.6 5.7 %constant_dynamic-update-slice_fusion.1 = (f32[8,52,16,128]{3,0,2,1:T(8,128)}, f32[8,52,16,128]{3,0,2,1:T(8,128)}, f32[8,56,16,128]{3,0,2,1:T(8,128)}) fusion(f32[8,48,16,128]{3,2,1,0:T(8,128)S(1)} %copy-done.1, f32[8,52,16,128]{3,0,2,1:T(8,128)} %get-tuple-element.55, f32[8,56,16,128]{3,0,2,1:T(8,128)} %get-tuple-element.56), kind=kLoop, calls=%fused_computation.168 | loop fusion | bytes 12582912
  42.0 5.8 %collective-permute-start.2 = (f32[8,56,4,128]{3,0,2,1:T(8,128)}, f32[8,56,4,128]{3,0,2,1:T(8,128)}, u32[]{:S(2)}, u32[]{:S(2)}) collective-permute-start(f32[8,56,4,128]{3,0,2,1:T(8,128)} %get-tuple-element.12), channel_id=1, source_target_pairs={{1,0},{2,1},{3,2},{4,3},{5,4},{6,5},{7,6},{0,7},{9,8},{10,9},{11,1... | collective-permute-start | bytes 2752520 | tf_op jit(solution)/shard_map/ppermute | solution.py:26
  51.7 5.6 %copy.105 = f32[8,48,16,1]{3,0,2,1:T(8,128)} copy(f32[8,48,16,1]{3,2,1,0:T(8,128)} %get-tuple-element.45) | data formatting | bytes 49152
  92.4 3.8 copy.116
  111.7 37.6 %fusion.43 = f32[8,48,16,128]{3,0,2,1:T(8,128)S(1)} fusion(f32[8,56,16,128]{3,0,2,1:T(8,128)} %get-tuple-element.54, f32[8,56,4,128]{3,0,2,1:T(8,128)} %collective-permute-done.3, f32[8,56,4,128]{3,0,2,1:T(8,128)} %collective-permute-done.2, f32[8,52,16,128]{3,0,2,1:T(8,128)} %get-tuple-element.49, f32[8,52,16,128]{3,0,2,1:T(8,128)} %get-tuple-element.53, ...), kind=kOutput, calls=%fused_computation.70 | convolution fusion | flops 128974848 | bytes 90440736 | tf_op jit(solution)/shard_map/kj,jxyz->kxyz/dot_general | solution.py:40
  153.1 3.8 fusion.100
  160.8 3.9 fusion.102
  171.2 3.9 fusion.104
  177.4 5.4 collective-permute-start.6
  187.0 3.9 fusion.106
  190.8 9.7 %collective-permute-done.6 = f32[8,56,4,128]{3,0,2,1:T(8,128)S(1)} collective-permute-done((f32[8,56,4,128]{3,0,2,1:T(8,128)S(1)}, f32[8,56,4,128]{3,0,2,1:T(8,128)S(1)}, u32[]{:S(2)}, u32[]{:S(2)}) %collective-permute-start.6) | collective-permute-done | bytes 917536 | tf_op jit(solution)/shard_map/ppermute | solution.py:26
  200.6 5.9 %collective-permute-done.7 = f32[8,56,4,128]{3,0,2,1:T(8,128)S(1)} collective-permute-done((f32[8,56,4,128]{3,0,2,1:T(8,128)S(1)}, f32[8,56,4,128]{3,0,2,1:T(8,128)S(1)}, u32[]{:S(2)}, u32[]{:S(2)}) %collective-permute-start.7) | collective-permute-done | bytes 917536 | tf_op jit(solution)/shard_map/ppermute | solution.py:25
  206.5 3.9 pad_maximum_fusion
  210.4 25.6 %fusion.117 = (bf16[8,48,16,128]{3,0,2,1:T(8,128)(2,1)S(1)}, f32[8,48,16,128]{3,0,2,1:T(8,128)}) fusion(f32[8,48,16,128]{3,0,2,1:T(8,128)S(1)} %fusion.43, f32[8,48,16,124]{3,0,2,1:T(8,128)} %get-tuple-element.16, f32[8,48,16,4]{3,0,2,1:T(8,128)} %get-tuple-element.14, f32[8]{0:T(128)S(1)} %get-tuple-element.62, f32[8,48,16,4]{3,0,2,1:T(8,128)} %get-tuple-element.15, ...), kind=kOutput, calls=%fused_computation.233 | convolution fusion | flops 131334144 | bytes 65028608 | tf_op jit(solution)/shard_map/kj,jxyz->kxyz/dot_general | solution.py:40
  237.9 10.6 %copy.90 = bf16[32,48,8,2,128]{4,3,2,1,0:T(2,128)(2,1)} copy(bf16[32,48,8,2,128]{4,0,3,1,2:T(8,128)(2,1)S(1)} %convert_bitcast_fusion) | data formatting | bytes 12582912 | tf_op jit(solution)/shard_map/convert_element_type | solution.py:89
  248.6 11.1 %reshape.133 = bf16[16,2,48,2048]{3,2,1,0:T(8,128)(2,1)} reshape(bf16[32,48,8,2,128]{4,3,2,1,0:T(2,128)(2,1)} %copy.90) | data formatting | bytes 12582912 | tf_op jit(solution)/shard_map/reshape | solution.py:91
  259.7 78.9 %all_to_all.15 = bf16[16,2,48,2048]{3,2,1,0:T(8,128)(2,1)S(1)} all-to-all(bf16[16,2,48,2048]{3,2,1,0:T(8,128)(2,1)} %reshape.133), channel_id=1, replica_groups=mesh['grp'=4,'gx'=4,'gy'=8] {'grp','gx'}, dimensions={0} | all-to-all | bytes 12582912 | tf_op jit(solution)/shard_map/all_to_all | solution.py:90
  342.4 6.5 %convolution_bitcast_fusion.1 = f32[768,768]{1,0:T(8,128)} fusion(bf16[2,768,2048]{2,1,0:T(8,128)(2,1)S(1)} %bitcast.95), kind=kOutput, calls=%fused_computation.147 | convolution fusion | flops 4831838208 | bytes 8650752 | tf_op jit(solution)/shard_map/dot_general | solution.py:98
  349.0 58.7 %all-reduce.3.cloned.1.call-done = f32[768,768]{1,0:T(8,128)} async-done(((f32[768,768]{1,0:T(8,128)}), f32[768,768]{1,0:T(8,128)}) %all-reduce.3.cloned.1.call-update) | async-done | bytes 2359312 | tf_op jit(solution)/shard_map/psum | solution.py:101
  410.0 108.6 %all-reduce.5.cloned.1.call-done = f32[768,768]{1,0:T(8,128)} async-done(((f32[768,768]{1,0:T(8,128)}), f32[768,768]{1,0:T(8,128)}) %all-reduce.5.cloned.1.call-update) | async-done | bytes 2359312 | tf_op jit(solution)/shard_map/psum | solution.py:101
  518.6 4.6 multiply_reduce_fusion
  528.2 4.0 convolution_bitcast_fusion
  (99 shorter events, 109.3 us)
Async XLA Ops:
  7.2 511.5 %copy-start = (f32[768,96]{0,1:T(8,128)S(1)}, f32[768,96]{0,1:T(8,128)}, u32[]{:S(2)}) copy-start(f32[768,96]{0,1:T(8,128)} %param.10) | copy-start | bytes 884740
  7.2 400.5 %all-reduce.3.cloned.1.call-start = ((), (), s32[]{:S(2)}) async-start(), calls=%async_computation.1 | async-start | bytes 4718592 | tf_op jit(solution)/shard_map/psum | solution.py:101
  9.2 21.6 %collective-permute-start.1 = (f32[8,4,16,128]{3,0,2,1:T(8,128)}, f32[8,4,16,128]{3,0,2,1:T(8,128)}, u32[]{:S(2)}, u32[]{:S(2)}) collective-permute-start(f32[8,4,16,128]{3,0,2,1:T(8,128)} %copy.103), channel_id=1, source_target_pairs={{0,8},{8,16},{16,24},{24,32},{32,40},{40,48},{48,56},{56,64},{64,7... | collective-permute-start | bytes 786440 | tf_op jit(solution)/shard_map/ppermute | solution.py:25
  13.1 5.8 %copy-start.1 = (f32[8,48,16,128]{3,2,1,0:T(8,128)S(1)}, f32[8,48,16,128]{3,2,1,0:T(8,128)}, u32[]{:S(2)}) copy-start(f32[8,48,16,128]{3,2,1,0:T(8,128)} %param.6) | copy-start | bytes 9437188
  13.1 25.2 %collective-permute-start = (f32[8,4,16,128]{3,0,2,1:T(8,128)}, f32[8,4,16,128]{3,0,2,1:T(8,128)S(1)}, u32[]{:S(2)}, u32[]{:S(2)}) collective-permute-start(f32[8,4,16,128]{3,0,2,1:T(8,128)} %copy.104), channel_id=1, source_target_pairs={{8,0},{16,8},{24,16},{32,24},{40,32},{48,40},{56,48},{64,56},{72,6... | collective-permute-start | bytes 786440 | tf_op jit(solution)/shard_map/ppermute | solution.py:26
  42.0 69.7 %collective-permute-start.2 = (f32[8,56,4,128]{3,0,2,1:T(8,128)}, f32[8,56,4,128]{3,0,2,1:T(8,128)}, u32[]{:S(2)}, u32[]{:S(2)}) collective-permute-start(f32[8,56,4,128]{3,0,2,1:T(8,128)} %get-tuple-element.12), channel_id=1, source_target_pairs={{1,0},{2,1},{3,2},{4,3},{5,4},{6,5},{7,6},{0,7},{9,8},{10,9},{11,1... | collective-permute-start | bytes 2752520 | tf_op jit(solution)/shard_map/ppermute | solution.py:26
  47.8 63.9 %collective-permute-start.3 = (f32[8,56,4,128]{3,0,2,1:T(8,128)}, f32[8,56,4,128]{3,0,2,1:T(8,128)}, u32[]{:S(2)}, u32[]{:S(2)}) collective-permute-start(f32[8,56,4,128]{3,0,2,1:T(8,128)} %get-tuple-element.13), channel_id=1, source_target_pairs={{0,1},{1,2},{2,3},{3,4},{4,5},{5,6},{6,7},{7,0},{8,9},{9,10},{10,1... | collective-permute-start | bytes 2752520 | tf_op jit(solution)/shard_map/ppermute | solution.py:25
  51.7 5.6 %copy-start.7 = (f32[8,48,16,127]{3,2,1,0:T(8,128)S(1)}, f32[8,48,16,127]{3,2,1,0:T(8,128)}, u32[]{:S(2)}) copy-start(f32[8,48,16,127]{3,2,1,0:T(8,128)} %get-tuple-element.47) | copy-start | bytes 9363460
  57.3 3.5 copy-start.6
  67.8 3.6 copy-start.5
  71.4 3.7 copy-start.4
  96.2 3.5 copy-start.9
  106.7 4.9 copy-start.13
  106.7 4.9 copy-start.14
  106.7 5.0 copy-start.15
  168.5 6.6 %collective-permute-start.4 = (f32[8,4,16,128]{3,0,2,1:T(8,128)S(1)}, f32[8,4,16,128]{3,0,2,1:T(8,128)S(1)}, u32[]{:S(2)}, u32[]{:S(2)}) collective-permute-start(f32[8,4,16,128]{3,0,2,1:T(8,128)S(1)} %get-tuple-element.30), channel_id=1, source_target_pairs={{8,0},{16,8},{24,16},{32,24},{40,32},{48,40},{56,48},{64,56},{72,6... | collective-permute-start | bytes 786440 | tf_op jit(solution)/shard_map/ppermute | solution.py:26
  171.2 6.0 %collective-permute-start.5 = (f32[8,4,16,128]{3,0,2,1:T(8,128)S(1)}, f32[8,4,16,128]{3,0,2,1:T(8,128)S(1)}, u32[]{:S(2)}, u32[]{:S(2)}) collective-permute-start(f32[8,4,16,128]{3,0,2,1:T(8,128)S(1)} %get-tuple-element.31), channel_id=1, source_target_pairs={{0,8},{8,16},{16,24},{24,32},{32,40},{40,48},{48,56},{56,64},{64,7... | collective-permute-start | bytes 786440 | tf_op jit(solution)/shard_map/ppermute | solution.py:25
  175.1 31.4 %copy-start.11 = (f32[8,4,16,128]{3,0,2,1:T(8,128)}, f32[8,4,16,128]{3,0,2,1:T(8,128)S(1)}, u32[]{:S(2)}) copy-start(f32[8,4,16,128]{3,0,2,1:T(8,128)S(1)} %collective-permute-done.4) | copy-start | bytes 786436
  177.2 29.3 %copy-start.12 = (f32[8,4,16,128]{3,0,2,1:T(8,128)}, f32[8,4,16,128]{3,0,2,1:T(8,128)S(1)}, u32[]{:S(2)}) copy-start(f32[8,4,16,128]{3,0,2,1:T(8,128)S(1)} %collective-permute-done.5) | copy-start | bytes 786436
  177.4 23.2 %collective-permute-start.6 = (f32[8,56,4,128]{3,0,2,1:T(8,128)S(1)}, f32[8,56,4,128]{3,0,2,1:T(8,128)S(1)}, u32[]{:S(2)}, u32[]{:S(2)}) collective-permute-start(f32[8,56,4,128]{3,0,2,1:T(8,128)S(1)} %get-tuple-element.10), channel_id=1, source_target_pairs={{1,0},{2,1},{3,2},{4,3},{5,4},{6,5},{7,6},{0,7},{9,8},{10,9},{11,1... | collective-permute-start | bytes 2752520 | tf_op jit(solution)/shard_map/ppermute | solution.py:26
  182.8 23.7 %collective-permute-start.7 = (f32[8,56,4,128]{3,0,2,1:T(8,128)S(1)}, f32[8,56,4,128]{3,0,2,1:T(8,128)S(1)}, u32[]{:S(2)}, u32[]{:S(2)}) collective-permute-start(f32[8,56,4,128]{3,0,2,1:T(8,128)S(1)} %get-tuple-element.11), channel_id=1, source_target_pairs={{0,1},{1,2},{2,3},{3,4},{4,5},{5,6},{6,7},{7,0},{8,9},{9,10},{10,1... | collective-permute-start | bytes 2752520 | tf_op jit(solution)/shard_map/ppermute | solution.py:25
  190.8 19.6 %copy-start.2 = (f32[8,48,16,128]{3,2,1,0:T(8,128)S(1)}, f32[8,48,16,128]{3,2,1,0:T(8,128)}, u32[]{:S(2)}) copy-start(f32[8,48,16,128]{3,2,1,0:T(8,128)} %param.6) | copy-start | bytes 9437188
  348.9 58.8 %copy-start.10 = (f32[8,48,16,128]{3,0,2,1:T(8,128)S(1)}, f32[8,48,16,128]{3,0,2,1:T(8,128)}, u32[]{:S(2)}) copy-start(f32[8,48,16,128]{3,0,2,1:T(8,128)} %get-tuple-element.83) | copy-start | bytes 9437188
  349.0 169.7 %all-reduce.5.cloned.1.call-start = ((), (), s32[]{:S(2)}) async-start(), calls=%async_computation.2 | async-start | bytes 4718592 | tf_op jit(solution)/shard_map/psum | solution.py:101
  (2 other events, 6.1 us)
Sparse Core Ops, SparseCore 0:
  349.1 58.5 all-reduce.2
  411.1 107.5 all-reduce.4
